TPU v7x, 32 devices: a whole 2x2x4 slice. The times are simulated.
32 devices in a mesh: harm: 4 (over z), pitch: 4 (over x, core), span: 2 (over y).
Axes of the slice: x: 2, y: 2, z: 4, core: 2. Of those that a mesh axis runs over, the one named last changes fastest.
Arguments:
- adjoint_start: float32 [16, 5, 32, 8, 256], P('harm', None, 'pitch', 'span'), may hold values from -6 to 6
- adjoint_source: float32 [16, 5, 32, 8, 256], P('harm', None, 'pitch', 'span'), may hold values from -6 to 6
- coupling: bfloat16 [16, 8, 5, 5, 32, 8, 256], P('harm', None, None, None, 'pitch', 'span'), may hold values from -0.796875 to 0.796875
- diag_inverse: bfloat16 [16, 5, 5, 32, 8, 256], P('harm', None, None, 'pitch', 'span'), may hold values from -0.25 to 0.80078125
- time_weight: float32 [32, 8, 256], P('pitch', 'span'), may hold values from 0.01 to 0.05
- pattern: int32 [32, 8, 8], P('pitch', 'span'), may hold values from 2 to 93, as said below
- face_match: int32 [8, 256], P('span'), may hold values from 0 to 255, each once within a row
- phase_index: int32 [1], replicated, may hold values from 1 to 23
Outputs:
- adjoint: float32 [16, 5, 32, 8, 256], P('harm', None, 'pitch', 'span')
Inputs may be any that keep to these rules, and one draw needn't show every extreme that they name: `pattern`: each tile's 8 entries name, in an order drawn for each tile, the tiles one and two places away from it pitchwise and spanwise, as row-major flat indices into its block's grid of (12) x (8) tiles, whose middle holds the block's own tiles. `face_match`: each row is a permutation of 0 to 255.
All inputs are finite; a program needn't handle non-finite values.
Results may differ from a plain program's by a relative error of at most 0.0003.
Values sent between devices are 32-bit elements; how exact they have to be, the bound alone decides.
A program may use at most 128 MiB of HBM per device.

v0:
```python
import functools
import math

import jax
import jax.numpy as jnp
import numpy as np
from jax import lax
from jax.experimental import pallas as pl
from jax.experimental.pallas import tpu as pltpu
from jax.sharding import PartitionSpec as P

BLADES = 24
SWEEPS = 2
MESH = pl.DeviceIdType.MESH
ORDER = (0, 3, 1, 2)


def to_rows(x):
    lead = x.shape[:-3]
    p, s, c = x.shape[-3:]
    x = x.reshape(lead + (p, s, c // 128, 128))
    x = jnp.swapaxes(x, -3, -2)
    return x.reshape(lead + (p * s * c // 128, 128))


def from_rows(x, p, s, c):
    lead = x.shape[:-2]
    x = x.reshape(lead + (p, c // 128, s, 128))
    x = jnp.swapaxes(x, -3, -2)
    return x.reshape(lead + (p, s, c))


def tables(n_samples, phase_index):
    j = np.arange(2 * n_samples) - n_samples
    d = j % n_samples
    safe = np.where(d == 0, 1, d)
    deriv = np.where(d == 0, 0.0, 0.5 * (-1.0) ** d / np.tan(np.pi * safe / n_samples))
    delta = 2.0 * math.pi * phase_index[0].astype(jnp.float32) / BLADES
    angle = jnp.asarray(2.0 * np.pi * d / n_samples, jnp.float32)[None, :]
    angle = angle + delta * jnp.asarray([[1.0], [-1.0]], jnp.float32)
    total = 1.0 + jnp.cos((n_samples // 2) * angle)
    for h in range(1, n_samples // 2):
        total = total + 2.0 * jnp.cos(h * angle)
    return jnp.concatenate([jnp.asarray(deriv, jnp.float32)[None], total / n_samples], axis=0)


def kernel(
    sizes,
    start_ref, source_ref, coupling_ref, diag_ref, weight_ref, pattern_ref, face_ref, tab_ref,
    out_ref,
    adj, src, coup_in, dinv, gath, raw, psend, left, right, coupled, codes, ptmp, onehot, rot2, rot4,
    load_sem, own_sem, zs_sem, zr_sem, rs_sem, rr_sem, ss_sem, sr_sem, ps_sem, pr_sem,
):
    n_loc, n_vars, n_slots, n_chunks, p_count, s_count = sizes
    f32 = jnp.float32
    h = lax.axis_index("harm")
    p = lax.axis_index("pitch")
    q = lax.axis_index("span")
    is_mid = (h == 1) | (h == 2)
    is_end = (h == 0) | (h == 3)
    pair = h + 1 - 2 * lax.rem(h, 2)
    other = 3 - h
    p_next = lax.rem(p + 1, p_count)
    p_prev = lax.rem(p + p_count - 1, p_count)
    has_left = q > 0
    has_right = q < s_count - 1

    loads = [
        pltpu.make_async_copy(start_ref, adj.at[0, :, :, pl.ds(16, 16 * n_chunks)], load_sem.at[0]),
        pltpu.make_async_copy(source_ref, src, load_sem.at[1]),
        pltpu.make_async_copy(diag_ref, dinv, load_sem.at[2]),
    ] + [
        pltpu.make_async_copy(coupling_ref.at[n], coup_in.at[n], load_sem.at[3 + n])
        for n in range(n_loc)
    ]
    for load in loads:
        load.start()

    barrier = pltpu.get_barrier_semaphore()

    def greet(dh, dp, dq):
        pl.semaphore_signal(barrier, inc=1, device_id=(dh, dp, dq), device_id_type=MESH)

    for step in range(1, 4):
        greet(lax.rem(h + step, 4), p, q)
    for dp in (p_next, p_prev):
        greet(h, dp, q)
        greet(pair, dp, q)

    @pl.when(has_left)
    def _():
        greet(h, p, q - 1)

    @pl.when(has_right)
    def _():
        greet(h, p, q + 1)

    pl.semaphore_wait(barrier, 7 + has_left.astype(jnp.int32) + has_right.astype(jnp.int32))

    def rows(c):
        return pl.ds(16 + 16 * c, 16)

    def remote(src_view, dst_view, send, recv, device):
        return pltpu.make_async_remote_copy(
            src_ref=src_view, dst_ref=dst_view, send_sem=send, recv_sem=recv,
            device_id=device, device_id_type=MESH,
        )

    def z_copy(s, c, slot, target):
        return remote(
            adj.at[s, :, :, rows(c)], gath.at[s, c, pl.ds(n_loc * h, n_loc)],
            zs_sem.at[s, c, slot], zr_sem.at[s, c, h], (target, p, q),
        )

    def raw_copy(s, c):
        return remote(
            psend.at[s, c], raw.at[s, c], rs_sem.at[s, c], rr_sem.at[s, c], (pair, p, q)
        )

    def span_copy(s, c, side):
        buf = right if side == 0 else left
        return remote(
            adj.at[s, :, :, rows(c)], buf.at[s, c], ss_sem.at[s, c, side], sr_sem.at[s, c, side],
            (h, p, q - 1 if side == 0 else q + 1),
        )

    def pitch_copy(s, side, src_view, slot, dh):
        dst = adj.at[s, :, :, pl.ds(16 + 16 * n_chunks, 16) if side == 0 else pl.ds(0, 16)]
        return remote(
            src_view, dst, ps_sem.at[s, side, slot], pr_sem.at[s, side],
            (dh, p_prev if side == 0 else p_next, q),
        )

    def plain_pitch(s, side):
        return pitch_copy(s, side, adj.at[s, :, :, rows(0 if side == 0 else n_chunks - 1)], 0, h)

    def rotated(side):
        return p == (0 if side == 0 else p_count - 1)

    def start_sends(s, c):
        @pl.when(is_end)
        def _():
            z_copy(s, c, 0, pair).start()
            z_copy(s, c, 1, 3 - pair).start()

        @pl.when(is_mid)
        def _():
            z_copy(s, c, 0, other).start()

        @pl.when(has_left)
        def _():
            span_copy(s, c, 0).start()

        @pl.when(has_right)
        def _():
            span_copy(s, c, 1).start()

        for side, edge in ((0, 0), (1, n_chunks - 1)):
            if c == edge:
                @pl.when(jnp.logical_not(rotated(side)))
                def _():
                    plain_pitch(s, side).start()

    loads[0].wait()
    for c in ORDER:
        start_sends(0, c)

    @pl.when(jnp.logical_not(has_left))
    def _():
        left[...] = jnp.zeros_like(left)

    @pl.when(jnp.logical_not(has_right))
    def _():
        right[...] = jnp.zeros_like(right)

    for pt in range(2 * n_chunks):
        val = pattern_ref[pt]
        col = lax.broadcasted_iota(jnp.int32, val.shape, 0)
        diff = val - ((pt + 2) * 8 + col + 2)
        code = jnp.zeros_like(diff)
        for number, step in enumerate((-16, -8, 8, 16, -2, -1, 1, 2)):
            code = jnp.where(diff == step, number, code)
        ptmp[pl.ds(8 * pt, 4), :] = code
        ptmp[pl.ds(8 * pt + 4, 4), :] = code
    for k in range(n_slots):
        codes[k] = jnp.broadcast_to(ptmp[:, k : k + 1], codes.shape[1:])

    @pl.when(is_mid & (rotated(0) | rotated(1)))
    def _():
        for sp in range(4):
            match = jnp.broadcast_to(face_ref[sp : sp + 1, :], (256, 256))
            cell = lax.broadcasted_iota(jnp.int32, (256, 256), 0)
            onehot[sp] = jnp.where(match == cell, 1.0, 0.0).astype(jnp.bfloat16)

    sub = lax.rem(lax.broadcasted_iota(jnp.int32, (16, 128), 0), 4)

    def halves(x, shift):
        return jnp.concatenate(
            [pltpu.roll(x[0:8], shift % 8, 0), pltpu.roll(x[8:16], shift % 8, 0)], axis=0
        )

    def span_step(x, lf, rt, step):
        if step < 0:
            return jnp.where(
                sub < -step, halves(lf, -step - 4), halves(x, -step)
            )
        return jnp.where(sub >= 4 - step, halves(rt, 4 - step), halves(x, -step))

    def couple(s, chunk_list):
        count = len(chunk_list)

        def one(i, carry):
            n = lax.rem(i, n_loc)
            c = jnp.int32(chunk_list[0])
            if count > 1:
                c = c + lax.div(i, n_loc) * (chunk_list[1] - chunk_list[0])
            at = pl.multiple_of(16 * c, 16)

            def over_w(w, acc):
                own = adj[s, n, w, pl.ds(at + 16, 16), :]
                lf = left[s, c, n, w]
                rt = right[s, c, n, w]
                cand = [
                    adj[s, n, w, pl.ds(at, 16), :],
                    adj[s, n, w, pl.ds(pl.multiple_of(at + 8, 8), 16), :],
                    adj[s, n, w, pl.ds(pl.multiple_of(at + 24, 8), 16), :],
                    adj[s, n, w, pl.ds(at + 32, 16), :],
                ] + [span_step(own, lf, rt, step) for step in (-2, -1, 1, 2)]
                acc = list(acc)
                for k in range(n_slots):
                    code = codes[k, pl.ds(at, 16), :]
                    m0 = (code & 1) != 0
                    m1 = (code & 2) != 0
                    m2 = code >= 4
                    pairs = [jnp.where(m0, cand[2 * i + 1], cand[2 * i]) for i in range(4)]
                    near = jnp.where(
                        m2, jnp.where(m1, pairs[3], pairs[2]), jnp.where(m1, pairs[1], pairs[0])
                    )
                    for v in range(n_vars):
                        acc[v] = acc[v] + coup_in[n, k, w, v, pl.ds(at, 16), :].astype(f32) * near
                return tuple(acc)

            acc = lax.fori_loop(
                0, n_vars, over_w, tuple(jnp.zeros((16, 128), f32) for _ in range(n_vars))
            )
            for v in range(n_vars):
                coupled[n, v, pl.ds(at, 16), :] = acc[v]
            return carry

        lax.fori_loop(0, n_loc * count, one, 0)

    def mix(s, c, row, group, store):
        first = 4 * n_loc - n_loc * group
        coef = {j: tab_ref[row, first + j] for j in range(1 - n_loc, 4 * n_loc)}

        def over_v(v, carry):
            x = [gath[s, c, m, v] for m in range(4 * n_loc)]
            for i in range(n_loc):
                acc = coef[-i] * x[0]
                for m in range(1, 4 * n_loc):
                    acc = acc + coef[m - i] * x[m]
                store(i, v, acc)
            return carry

        lax.fori_loop(0, n_vars, over_v, 0)

    def turn(s, side):
        c = 0 if side == 0 else n_chunks - 1
        block = n_loc * n_vars * 16
        for which, group in ((0, h), (1, pair)):
            def put(i, v, value, which=which):
                at = pl.multiple_of(which * block + (i * n_vars + v) * 16, 16)
                rot2[pl.ds(at, 16), :] = value

            mix(s, c, 1 + side, group, put)
        count = 2 * block // 8
        for sp in range(4):
            x = jnp.concatenate(
                [rot2[pl.ds(cb * 4 + sp, count, stride=8), :] for cb in range(2)], axis=1
            )
            total = jnp.zeros((count, 256), f32)
            for _ in range(3):
                part = x.astype(jnp.bfloat16)
                x = x - part.astype(f32)
                dims = (((1,), (1,)), ((), ())) if side == 0 else (((1,), (0,)), ((), ()))
                total = total + lax.dot_general(
                    part, onehot[sp], dims, preferred_element_type=f32
                )
            for cb in range(2):
                rot2[pl.ds(cb * 4 + sp, count, stride=8), :] = total[:, 128 * cb : 128 * cb + 128]
        for which in range(2):
            for i in range(n_loc):
                for v in range(n_vars):
                    at = which * block + (i * n_vars + v) * 16
                    rot4[s, which, i, v] = rot2[pl.ds(at, 16), :]
        pitch_copy(s, side, rot4.at[s, 0], 0, h).start()
        pitch_copy(s, side, rot4.at[s, 1], 1, pair).start()

    def times(s, c):
        @pl.when(is_mid)
        def _():
            own = pltpu.make_async_copy(
                adj.at[s, :, :, rows(c)], gath.at[s, c, pl.ds(n_loc * h, n_loc)], own_sem
            )
            own.start()
            own.wait()
            for dh in (pair, other, 3 - pair):
                remote(
                    adj.at[s, :, :, rows(c)], gath.at[s, c, pl.ds(n_loc * dh, n_loc)],
                    zs_sem.at[s, c, 0], zr_sem.at[s, c, dh], (dh, p, q),
                ).wait_recv()

            def put_pair(i, v, value):
                psend[s, c, i, v] = value

            def put_own(i, v, value):
                raw[s, c, i, v] = value

            mix(s, c, 0, pair, put_pair)
            raw_copy(s, c).start()
            for side, edge in ((0, 0), (1, n_chunks - 1)):
                if c == edge:
                    @pl.when(rotated(side))
                    def _():
                        turn(s, side)
            mix(s, c, 0, h, put_own)

    def finish(s, c):
        @pl.when(is_end)
        def _():
            raw_copy(s, c).wait_recv()

        def one(n, carry):
            weight = weight_ref[pl.ds(16 * c, 16), :]
            acc = [jnp.zeros((16, 128), f32) for _ in range(n_vars)]
            for w in range(n_vars):
                balance = (
                    src[n, w, pl.ds(16 * c, 16), :]
                    - coupled[n, w, pl.ds(16 * c, 16), :]
                    - weight * raw[s, c, n, w]
                )
                for v in range(n_vars):
                    acc[v] = acc[v] + dinv[n, w, v, pl.ds(16 * c, 16), :].astype(f32) * balance
            for v in range(n_vars):
                if s + 1 < SWEEPS:
                    adj[s + 1, n, v, rows(c), :] = acc[v]
                else:
                    out_ref[n, v, pl.ds(16 * c, 16), :] = acc[v]
            return carry

        lax.fori_loop(0, n_loc, one, 0)
        if s + 1 < SWEEPS:
            start_sends(s + 1, c)

    def wait_span(s, c):
        @pl.when(has_right)
        def _():
            span_copy(s, c, 0).wait_recv()

        @pl.when(has_left)
        def _():
            span_copy(s, c, 1).wait_recv()

    for load in loads[1:]:
        load.wait()
    for s in range(SWEEPS):
        if s > 0:
            times(s, 0)
            times(s, n_chunks - 1)
        for c in ORDER[2:]:
            wait_span(s, c)
        couple(s, ORDER[2:])
        if s == 0:
            times(s, 0)
            times(s, n_chunks - 1)
        for c in ORDER[:2]:
            wait_span(s, c)
        for side in range(2):
            plain_pitch(s, side).wait_recv()
        couple(s, ORDER[:2])
        finish(s, ORDER[0])
        finish(s, ORDER[1])
        for c in ORDER[2:]:
            times(s, c)
            finish(s, c)

    for s in range(SWEEPS):
        for c in range(n_chunks):
            @pl.when(is_end)
            def _():
                z_copy(s, c, 0, pair).wait_send()
                z_copy(s, c, 1, 3 - pair).wait_send()

            @pl.when(is_mid)
            def _():
                z_copy(s, c, 0, other).wait_send()
                raw_copy(s, c).wait_send()

            @pl.when(has_left)
            def _():
                span_copy(s, c, 0).wait_send()

            @pl.when(has_right)
            def _():
                span_copy(s, c, 1).wait_send()

        for side in range(2):
            @pl.when(jnp.logical_not(rotated(side)))
            def _():
                plain_pitch(s, side).wait_send()

            @pl.when(rotated(side) & is_mid)
            def _():
                pitch_copy(s, side, rot4.at[s, 0], 0, h).wait_send()
                pitch_copy(s, side, rot4.at[s, 1], 1, pair).wait_send()


def local(
    adjoint_start, adjoint_source, coupling, diag_inverse, time_weight, pattern, face_match, phase_index
):
    n_loc, n_vars, p_tiles, s_tiles, line = adjoint_start.shape
    n_slots = pattern.shape[2]
    h_count = lax.axis_size("harm")
    p_count = lax.axis_size("pitch")
    s_count = lax.axis_size("span")
    assert h_count == 4 and s_tiles * line == 1024 and n_slots == 8 and p_count > 2
    n_rows = p_tiles * 8
    n_chunks = p_tiles // 2
    sizes = (n_loc, n_vars, n_slots, n_chunks, p_count, s_count)
    f32, bf16 = jnp.float32, jnp.bfloat16
    hbm = pl.BlockSpec(memory_space=pl.ANY)
    vmem = pl.BlockSpec(memory_space=pltpu.VMEM)
    smem = pl.BlockSpec(memory_space=pltpu.SMEM)
    dma = pltpu.SemaphoreType.DMA
    part = (n_loc, n_vars, 16, 128)
    out = pl.pallas_call(
        functools.partial(kernel, sizes),
        out_shape=jax.ShapeDtypeStruct((n_loc, n_vars, n_rows, 128), f32),
        in_specs=[hbm, hbm, hbm, hbm, vmem, vmem, vmem, smem],
        out_specs=vmem,
        scratch_shapes=[
            pltpu.VMEM((SWEEPS, n_loc, n_vars, n_rows + 32, 128), f32),
            pltpu.VMEM((n_loc, n_vars, n_rows, 128), f32),
            pltpu.VMEM((n_loc, n_slots, n_vars, n_vars, n_rows, 128), bf16),
            pltpu.VMEM((n_loc, n_vars, n_vars, n_rows, 128), bf16),
            pltpu.VMEM((SWEEPS, n_chunks, 4 * n_loc, n_vars, 16, 128), f32),
            pltpu.VMEM((SWEEPS, n_chunks) + part, f32),
            pltpu.VMEM((SWEEPS, n_chunks) + part, f32),
            pltpu.VMEM((SWEEPS, n_chunks) + part, f32),
            pltpu.VMEM((SWEEPS, n_chunks) + part, f32),
            pltpu.VMEM((n_loc, n_vars, n_rows, 128), f32),
            pltpu.VMEM((n_slots, n_rows, 128), jnp.int32),
            pltpu.VMEM((n_rows, n_slots), jnp.int32),
            pltpu.VMEM((4, 256, 256), bf16),
            pltpu.VMEM((2 * n_loc * n_vars * 16, 128), f32),
            pltpu.VMEM((SWEEPS, 2) + part, f32),
            dma((3 + n_loc,)),
            dma,
            dma((SWEEPS, n_chunks, 2)),
            dma((SWEEPS, n_chunks, 4)),
            dma((SWEEPS, n_chunks)),
            dma((SWEEPS, n_chunks)),
            dma((SWEEPS, n_chunks, 2)),
            dma((SWEEPS, n_chunks, 2)),
            dma((SWEEPS, 2, 2)),
            dma((SWEEPS, 2)),
        ],
        compiler_params=pltpu.CompilerParams(
            collective_id=0, has_side_effects=True, vmem_limit_bytes=48 * 1024 * 1024
        ),
        cost_estimate=pl.CostEstimate(flops=40_000_000, bytes_accessed=18_000_000, transcendentals=0),
    )(
        to_rows(adjoint_start),
        to_rows(adjoint_source),
        to_rows(coupling),
        to_rows(diag_inverse),
        to_rows(time_weight),
        pattern,
        face_match,
        tables(n_loc * h_count, phase_index),
    )
    return from_rows(out, p_tiles, s_tiles, line)


def solution(mesh):
    placed = (
        P("harm", None, "pitch", "span", None),
        P("harm", None, "pitch", "span", None),
        P("harm", None, None, None, "pitch", "span", None),
        P("harm", None, None, "pitch", "span", None),
        P("pitch", "span", None),
        P("pitch", "span", None),
        P("span", None),
        P(),
    )
    return jax.shard_map(
        local,
        mesh=mesh,
        in_specs=placed,
        out_specs=P("harm", None, "pitch", "span", None),
        check_vma=False,
    )
```

profile of v0, /device:TPU:0, one launch (start us, length us, event | category | flops | bytes accessed | tf_op | source)
XLA Modules:
  0.0 80.4 jit_solution(361009195179308358)
XLA Ops:
  0.7 0.7 multiply_bitcast_fusion
  1.3 0.8 %fusion.20 = f32[2,32]{1,0:T(2,128)S(1)} fusion(f32[32]{0:T(128)} %constant.31.clone, f32[2]{0:T(128)S(1)} %multiply_bitcast_fusion), kind=kLoop, calls=%fused_computation.29 | loop fusion | flops 1536 | bytes 392 | tf_op jit(solution)/shard_map/div | solution.py:44
  2.2 0.7 pad_maximum_fusion.tab_ref
  2.8 0.0 copy-start
  2.8 1.4 %copy-done = bf16[4,5,5,8,4,256]{5,4,3,2,1,0:T(4,128)(2,1)S(1)} copy-done((bf16[4,5,5,8,4,256]{5,4,3,2,1,0:T(4,128)(2,1)S(1)}, bf16[4,5,5,8,4,256]{5,4,3,2,1,0:T(4,128)(2,1)}, u32[]{:S(2)}) %copy-start) | copy-done | bytes 1638424
  4.3 0.0 copy-start.1
  4.3 1.1 %copy-done.1 = f32[4,5,8,4,256]{4,3,2,1,0:T(4,128)S(1)} copy-done((f32[4,5,8,4,256]{4,3,2,1,0:T(4,128)S(1)}, f32[4,5,8,4,256]{4,3,2,1,0:T(4,128)}, u32[]{:S(2)}) %copy-start.1) | copy-done | bytes 655384
  5.3 0.0 copy-start.2
  5.3 1.1 %copy-done.2 = f32[4,5,8,4,256]{4,3,2,1,0:T(4,128)S(1)} copy-done((f32[4,5,8,4,256]{4,3,2,1,0:T(4,128)S(1)}, f32[4,5,8,4,256]{4,3,2,1,0:T(4,128)}, u32[]{:S(2)}) %copy-start.2) | copy-done | bytes 655384
  6.4 0.0 copy-start.3
  6.4 0.8 copy-done.3
  7.2 0.0 copy-start.4
  7.2 0.7 copy-done.4
  7.9 0.0 copy-start.5
  7.9 0.7 copy-done.5
  8.6 70.9 %shard_map.109 = f32[4,5,64,128]{3,2,1,0:T(8,128)S(1)} custom-call(f32[4,5,64,128]{3,2,1,0:T(8,128)S(1)} %bitcast.35, f32[4,5,64,128]{3,2,1,0:T(8,128)S(1)} %bitcast.36, bf16[4,8,5,5,64,128]{5,4,3,2,1,0:T(8,128)(2,1)} %bitcast.38, bf16[4,5,5,64,128]{4,3,2,1,0:T(8,128)(2,1)S(1)} %bitcast.34, f32[64,128]{1,0:T(8,128)S(1)} %bitcast.37, ...), custom_call_target="tpu_custom_call" | custom-call | flops 40000000 | bytes 18000000 | tf_op jit(solution)/shard_map/pallas_call | solution.py:436
  79.6 0.8 %copy.20 = f32[4,5,8,4,256]{4,3,2,1,0:T(4,128)} copy(f32[4,5,8,4,256]{4,3,2,1,0:T(4,128)S(1)} %bitcast.33) | data formatting | bytes 1310720
Async XLA Ops:
  2.8 1.4 %copy-start = (bf16[4,5,5,8,4,256]{5,4,3,2,1,0:T(4,128)(2,1)S(1)}, bf16[4,5,5,8,4,256]{5,4,3,2,1,0:T(4,128)(2,1)}, u32[]{:S(2)}) copy-start(bf16[4,5,5,8,4,256]{5,4,3,2,1,0:T(4,128)(2,1)} %param.14) | copy-start | bytes 4915204
  4.3 1.1 %copy-start.1 = (f32[4,5,8,4,256]{4,3,2,1,0:T(4,128)S(1)}, f32[4,5,8,4,256]{4,3,2,1,0:T(4,128)}, u32[]{:S(2)}) copy-start(f32[4,5,8,4,256]{4,3,2,1,0:T(4,128)} %param.11) | copy-start | bytes 1966084
  5.3 1.1 %copy-start.2 = (f32[4,5,8,4,256]{4,3,2,1,0:T(4,128)S(1)}, f32[4,5,8,4,256]{4,3,2,1,0:T(4,128)}, u32[]{:S(2)}) copy-start(f32[4,5,8,4,256]{4,3,2,1,0:T(4,128)} %param.12) | copy-start | bytes 1966084
  6.4 0.8 copy-start.3
  7.2 0.7 copy-start.4
  7.9 0.7 copy-start.5
where the time goes:
time: 80.8 us; the launch traced here: 80.4 us
  Pallas kernels  70.9 us (88%)
  local copies, waits for them, and re-layouts  6.6 us (8%)
  other arithmetic  2.17 us (3%)
    pallas_call x1, Pallas kernels, local(): pl.pallas_call(functools.partial(kernel, sizes), out_shape=jax.ShapeDtype...  70.9 us
    unnamed x13, local copies, waits for them, and re-layouts  6.6 us

commit v1 on v0

--- a/solution.py
+++ b/solution.py
@@ -30,25 +30,19 @@
     return x.reshape(lead + (p, s, c))
 
 
-def tables(n_samples, phase_index):
-    j = np.arange(2 * n_samples) - n_samples
-    d = j % n_samples
+def derivative_values(n_samples):
+    d = np.arange(n_samples)
     safe = np.where(d == 0, 1, d)
-    deriv = np.where(d == 0, 0.0, 0.5 * (-1.0) ** d / np.tan(np.pi * safe / n_samples))
-    delta = 2.0 * math.pi * phase_index[0].astype(jnp.float32) / BLADES
-    angle = jnp.asarray(2.0 * np.pi * d / n_samples, jnp.float32)[None, :]
-    angle = angle + delta * jnp.asarray([[1.0], [-1.0]], jnp.float32)
-    total = 1.0 + jnp.cos((n_samples // 2) * angle)
-    for h in range(1, n_samples // 2):
-        total = total + 2.0 * jnp.cos(h * angle)
-    return jnp.concatenate([jnp.asarray(deriv, jnp.float32)[None], total / n_samples], axis=0)
+    values = np.where(d == 0, 0.0, 0.5 * (-1.0) ** d / np.tan(np.pi * safe / n_samples))
+    return [float(v) for v in values]
 
 
 def kernel(
     sizes,
-    start_ref, source_ref, coupling_ref, diag_ref, weight_ref, pattern_ref, face_ref, tab_ref,
+    start_ref, source_ref, coupling_ref, diag_ref, weight_hbm, pattern_hbm, face_hbm, phase_ref,
     out_ref,
     adj, src, coup_in, dinv, gath, raw, psend, left, right, coupled, codes, ptmp, onehot, rot2, rot4,
+    weight_ref, pattern_ref, face_ref, deriv, vtmp, rtab,
     load_sem, own_sem, zs_sem, zr_sem, rs_sem, rr_sem, ss_sem, sr_sem, ps_sem, pr_sem,
 ):
     n_loc, n_vars, n_slots, n_chunks, p_count, s_count = sizes
@@ -69,8 +63,11 @@
         pltpu.make_async_copy(start_ref, adj.at[0, :, :, pl.ds(16, 16 * n_chunks)], load_sem.at[0]),
         pltpu.make_async_copy(source_ref, src, load_sem.at[1]),
         pltpu.make_async_copy(diag_ref, dinv, load_sem.at[2]),
+        pltpu.make_async_copy(weight_hbm, weight_ref, load_sem.at[3]),
+        pltpu.make_async_copy(pattern_hbm, pattern_ref, load_sem.at[4]),
+        pltpu.make_async_copy(face_hbm, face_ref, load_sem.at[5]),
     ] + [
-        pltpu.make_async_copy(coupling_ref.at[n], coup_in.at[n], load_sem.at[3 + n])
+        pltpu.make_async_copy(coupling_ref.at[n], coup_in.at[n], load_sem.at[6 + n])
         for n in range(n_loc)
     ]
     for load in loads:
@@ -106,21 +103,32 @@
             device_id=device, device_id_type=MESH,
         )
 
-    def z_copy(s, c, slot, target):
+    def chunk(s, c, v=slice(None)):
+        return adj.at[s, :, v, rows(c)]
+
+    def z_copy(s, c, v, slot, target):
         return remote(
-            adj.at[s, :, :, rows(c)], gath.at[s, c, pl.ds(n_loc * h, n_loc)],
-            zs_sem.at[s, c, slot], zr_sem.at[s, c, h], (target, p, q),
+            chunk(s, c, v), gath.at[s, c, pl.ds(n_loc * h, n_loc), v],
+            zs_sem.at[s, c, v, slot], zr_sem.at[s, c, v, h], (target, p, q),
         )
 
-    def raw_copy(s, c):
+    def raw_copy(s, c, v):
         return remote(
-            psend.at[s, c], raw.at[s, c], rs_sem.at[s, c], rr_sem.at[s, c], (pair, p, q)
+            psend.at[s, c, :, v], raw.at[s, c, :, v], rs_sem.at[s, c, v], rr_sem.at[s, c, v],
+            (pair, p, q),
         )
+
+    def each_v(body):
+        def step(v, carry):
+            body(v)
+            return carry
+
+        lax.fori_loop(0, n_vars, step, 0)
 
     def span_copy(s, c, side):
         buf = right if side == 0 else left
         return remote(
-            adj.at[s, :, :, rows(c)], buf.at[s, c], ss_sem.at[s, c, side], sr_sem.at[s, c, side],
+            chunk(s, c), buf.at[s, c], ss_sem.at[s, c, side], sr_sem.at[s, c, side],
             (h, p, q - 1 if side == 0 else q + 1),
         )
 
@@ -132,20 +140,38 @@
         )
 
     def plain_pitch(s, side):
-        return pitch_copy(s, side, adj.at[s, :, :, rows(0 if side == 0 else n_chunks - 1)], 0, h)
+        return pitch_copy(s, side, chunk(s, 0 if side == 0 else n_chunks - 1), 0, h)
 
     def rotated(side):
         return p == (0 if side == 0 else p_count - 1)
 
+    def start_z(s, c):
+        @pl.when(is_end)
+        def _():
+            def send(v):
+                z_copy(s, c, v, 0, 3 - pair).start()
+                z_copy(s, c, v, 1, pair).start()
+
+            each_v(send)
+
+        @pl.when(is_mid)
+        def _():
+            each_v(lambda v: z_copy(s, c, v, 0, other).start())
+
+    def wait_z(s, c):
+        @pl.when(is_end)
+        def _():
+            def wait(v):
+                z_copy(s, c, v, 0, 3 - pair).wait_send()
+                z_copy(s, c, v, 1, pair).wait_send()
+
+            each_v(wait)
+
+        @pl.when(is_mid)
+        def _():
+            each_v(lambda v: z_copy(s, c, v, 0, other).wait_send())
+
     def start_sends(s, c):
-        @pl.when(is_end)
-        def _():
-            z_copy(s, c, 0, pair).start()
-            z_copy(s, c, 1, 3 - pair).start()
-
-        @pl.when(is_mid)
-        def _():
-            z_copy(s, c, 0, other).start()
 
         @pl.when(has_left)
         def _():
@@ -163,7 +189,27 @@
 
     loads[0].wait()
     for c in ORDER:
+        start_z(0, c)
+    for c in ORDER:
         start_sends(0, c)
+    for load in loads[1:6]:
+        load.wait()
+
+    for j, value in enumerate(2 * derivative_values(4 * n_loc)):
+        deriv[j] = jnp.float32(value)
+
+    @pl.when(is_mid & (rotated(0) | rotated(1)))
+    def _():
+        n_all = 4 * n_loc
+        delta = jnp.broadcast_to(phase_ref[0], (8, 128)).astype(f32) * (2.0 * math.pi / BLADES)
+        d = lax.rem(lax.broadcasted_iota(jnp.int32, (8, 128), 1), n_all).astype(f32)
+        angle = d * (2.0 * math.pi / n_all) + delta
+        total = 1.0 + jnp.cos((n_all // 2) * angle)
+        for m in range(1, n_all // 2):
+            total = total + 2.0 * jnp.cos(m * angle)
+        vtmp[...] = total / n_all
+        for j in range(2 * n_all):
+            rtab[j] = jnp.broadcast_to(vtmp[:, j % n_all : j % n_all + 1], (8, 128))
 
     @pl.when(jnp.logical_not(has_left))
     def _():
@@ -249,20 +295,26 @@
 
         lax.fori_loop(0, n_loc * count, one, 0)
 
-    def mix(s, c, row, group, store):
+    def mix(s, c, v, group, coef, store):
         first = 4 * n_loc - n_loc * group
-        coef = {j: tab_ref[row, first + j] for j in range(1 - n_loc, 4 * n_loc)}
-
-        def over_v(v, carry):
-            x = [gath[s, c, m, v] for m in range(4 * n_loc)]
-            for i in range(n_loc):
-                acc = coef[-i] * x[0]
-                for m in range(1, 4 * n_loc):
-                    acc = acc + coef[m - i] * x[m]
-                store(i, v, acc)
-            return carry
-
-        lax.fori_loop(0, n_vars, over_v, 0)
+        values = {j: coef(first, j) for j in range(1 - n_loc, 4 * n_loc)}
+        x = [gath[s, c, m, v] for m in range(4 * n_loc)]
+        for i in range(n_loc):
+            acc = values[-i] * x[0]
+            for m in range(1, 4 * n_loc):
+                acc = acc + values[m - i] * x[m]
+            store(i, v, acc)
+
+    def time_coef(first, j):
+        return deriv[first + j]
+
+    def low_coef(first, j):
+        t = rtab[first + j]
+        return jnp.concatenate([t, t], axis=0)
+
+    def high_coef(first, j):
+        t = rtab[8 * n_loc - first - j]
+        return jnp.concatenate([t, t], axis=0)
 
     def turn(s, side):
         c = 0 if side == 0 else n_chunks - 1
@@ -272,7 +324,8 @@
                 at = pl.multiple_of(which * block + (i * n_vars + v) * 16, 16)
                 rot2[pl.ds(at, 16), :] = value
 
-            mix(s, c, 1 + side, group, put)
+            coef = low_coef if side == 0 else high_coef
+            each_v(lambda v, put=put, group=group: mix(s, c, v, group, coef, put))
         count = 2 * block // 8
         for sp in range(4):
             x = jnp.concatenate(
@@ -300,15 +353,10 @@
         @pl.when(is_mid)
         def _():
             own = pltpu.make_async_copy(
-                adj.at[s, :, :, rows(c)], gath.at[s, c, pl.ds(n_loc * h, n_loc)], own_sem
+                chunk(s, c), gath.at[s, c, pl.ds(n_loc * h, n_loc)], own_sem
             )
             own.start()
             own.wait()
-            for dh in (pair, other, 3 - pair):
-                remote(
-                    adj.at[s, :, :, rows(c)], gath.at[s, c, pl.ds(n_loc * dh, n_loc)],
-                    zs_sem.at[s, c, 0], zr_sem.at[s, c, dh], (dh, p, q),
-                ).wait_recv()
 
             def put_pair(i, v, value):
                 psend[s, c, i, v] = value
@@ -316,19 +364,27 @@
             def put_own(i, v, value):
                 raw[s, c, i, v] = value
 
-            mix(s, c, 0, pair, put_pair)
-            raw_copy(s, c).start()
+            def relay(v):
+                for dh in (pair, other, 3 - pair):
+                    remote(
+                        chunk(s, c, v), gath.at[s, c, pl.ds(n_loc * dh, n_loc), v],
+                        zs_sem.at[s, c, v, 0], zr_sem.at[s, c, v, dh], (dh, p, q),
+                    ).wait_recv()
+                mix(s, c, v, pair, time_coef, put_pair)
+                raw_copy(s, c, v).start()
+
+            each_v(relay)
             for side, edge in ((0, 0), (1, n_chunks - 1)):
                 if c == edge:
                     @pl.when(rotated(side))
                     def _():
                         turn(s, side)
-            mix(s, c, 0, h, put_own)
+            each_v(lambda v: mix(s, c, v, h, time_coef, put_own))
 
     def finish(s, c):
         @pl.when(is_end)
         def _():
-            raw_copy(s, c).wait_recv()
+            each_v(lambda v: raw_copy(s, c, v).wait_recv())
 
         def one(n, carry):
             weight = weight_ref[pl.ds(16 * c, 16), :]
@@ -350,6 +406,7 @@
 
         lax.fori_loop(0, n_loc, one, 0)
         if s + 1 < SWEEPS:
+            start_z(s + 1, c)
             start_sends(s + 1, c)
 
     def wait_span(s, c):
@@ -361,7 +418,7 @@
         def _():
             span_copy(s, c, 1).wait_recv()
 
-    for load in loads[1:]:
+    for load in loads[6:]:
         load.wait()
     for s in range(SWEEPS):
         if s > 0:
@@ -386,15 +443,11 @@
 
     for s in range(SWEEPS):
         for c in range(n_chunks):
-            @pl.when(is_end)
-            def _():
-                z_copy(s, c, 0, pair).wait_send()
-                z_copy(s, c, 1, 3 - pair).wait_send()
+            wait_z(s, c)
 
             @pl.when(is_mid)
             def _():
-                z_copy(s, c, 0, other).wait_send()
-                raw_copy(s, c).wait_send()
+                each_v(lambda v: raw_copy(s, c, v).wait_send())
 
             @pl.when(has_left)
             def _():
@@ -430,13 +483,12 @@
     f32, bf16 = jnp.float32, jnp.bfloat16
     hbm = pl.BlockSpec(memory_space=pl.ANY)
     vmem = pl.BlockSpec(memory_space=pltpu.VMEM)
-    smem = pl.BlockSpec(memory_space=pltpu.SMEM)
     dma = pltpu.SemaphoreType.DMA
     part = (n_loc, n_vars, 16, 128)
     out = pl.pallas_call(
         functools.partial(kernel, sizes),
         out_shape=jax.ShapeDtypeStruct((n_loc, n_vars, n_rows, 128), f32),
-        in_specs=[hbm, hbm, hbm, hbm, vmem, vmem, vmem, smem],
+        in_specs=[hbm] * 7 + [pl.BlockSpec(memory_space=pltpu.SMEM)],
         out_specs=vmem,
         scratch_shapes=[
             pltpu.VMEM((SWEEPS, n_loc, n_vars, n_rows + 32, 128), f32),
@@ -454,19 +506,25 @@
             pltpu.VMEM((4, 256, 256), bf16),
             pltpu.VMEM((2 * n_loc * n_vars * 16, 128), f32),
             pltpu.VMEM((SWEEPS, 2) + part, f32),
-            dma((3 + n_loc,)),
+            pltpu.VMEM((n_rows, 128), f32),
+            pltpu.VMEM(pattern.shape, jnp.int32),
+            pltpu.VMEM(face_match.shape, jnp.int32),
+            pltpu.SMEM((8 * n_loc,), f32),
+            pltpu.VMEM((8, 128), f32),
+            pltpu.VMEM((8 * n_loc, 8, 128), f32),
+            dma((6 + n_loc,)),
             dma,
-            dma((SWEEPS, n_chunks, 2)),
-            dma((SWEEPS, n_chunks, 4)),
-            dma((SWEEPS, n_chunks)),
-            dma((SWEEPS, n_chunks)),
+            dma((SWEEPS, n_chunks, n_vars, 2)),
+            dma((SWEEPS, n_chunks, n_vars, 4)),
+            dma((SWEEPS, n_chunks, n_vars)),
+            dma((SWEEPS, n_chunks, n_vars)),
             dma((SWEEPS, n_chunks, 2)),
             dma((SWEEPS, n_chunks, 2)),
             dma((SWEEPS, 2, 2)),
             dma((SWEEPS, 2)),
         ],
         compiler_params=pltpu.CompilerParams(
-            collective_id=0, has_side_effects=True, vmem_limit_bytes=48 * 1024 * 1024
+            collective_id=0, has_side_effects=True, vmem_limit_bytes=60 * 1024 * 1024
         ),
         cost_estimate=pl.CostEstimate(flops=40_000_000, bytes_accessed=18_000_000, transcendentals=0),
     )(
@@ -477,7 +535,7 @@
         to_rows(time_weight),
         pattern,
         face_match,
-        tables(n_loc * h_count, phase_index),
+        phase_index,
     )
     return from_rows(out, p_tiles, s_tiles, line)
 

time: 80.8 us -> 75.3 us (0.932)
  local copies, waits for them, and re-layouts: 6.6 us -> 2.09 us
  other arithmetic: 2.17 us -> 0 us
  Pallas kernels: 70.9 us -> 72.4 us
    unnamed x13 -> x1, local copies, waits for them, and re-layouts: 6.6 us -> 2.09 us
    pallas_call x1, Pallas kernels: 70.9 us -> 72.4 us  [local(): pl.pallas_call(functools.partial(kernel, sizes), out_shape=jax.ShapeDtype...]
    div x1 -> x0, other arithmetic: 0.84 us -> none  [tables(): total / n_samples]
where the time goes in v1:
time: 75.3 us; the launch traced here: 75.1 us
  Pallas kernels  72.4 us (96%)
  local copies, waits for them, and re-layouts  2.09 us (3%)
    pallas_call x1, Pallas kernels, local(): pl.pallas_call(functools.partial(kernel, sizes), out_shape=jax.ShapeDtype...  72.4 us
    unnamed x1, local copies, waits for them, and re-layouts  2.09 us

profile of v1, /device:TPU:0, one launch (start us, length us, event | category | flops | bytes accessed | tf_op | source)
XLA Modules:
  0.0 75.1 jit_solution(5279743482717086936)
XLA Ops:
  0.7 72.4 %shard_map.82 = f32[4,5,64,128]{3,2,1,0:T(8,128)} custom-call(f32[4,5,64,128]{3,2,1,0:T(8,128)} %bitcast.33, f32[4,5,64,128]{3,2,1,0:T(8,128)} %bitcast.34, bf16[4,8,5,5,64,128]{5,4,3,2,1,0:T(8,128)(2,1)} %bitcast.30, bf16[4,5,5,64,128]{4,3,2,1,0:T(8,128)(2,1)} %bitcast.32, f32[64,128]{1,0:T(8,128)} %bitcast.35, s32[8,4,8]{2,1,0:T(4,128)} %pattern_hbm.1, ...), custom_call_target="tpu_custom_call" | custom-call | flops 40000000 | bytes 18000000 | tf_op jit(solution)/shard_map/pallas_call | solution.py:488
  73.0 2.1 %copy.17 = f32[4,5,8,4,256]{4,3,2,1,0:T(4,128)} copy(f32[4,5,8,4,256]{4,3,2,1,0:T(4,128)} %bitcast.31) | data formatting | bytes 1310720
